TPU v7x, 128 devices: a whole 4x4x4 slice. The times are simulated.
128 devices in a mesh: section: 2 (over core), tp: 64 (over z, y, x).
Axes of the slice: x: 4, y: 4, z: 4, core: 2. Of those that a mesh axis runs over, the one named last changes fastest.
Arguments:
- incoming_hidden_states: bfloat16 [16, 8192], replicated, may hold values from -6 to 6
- parent_positions: int32 [16], replicated, may hold values from 0 to 15
- filled_extents: int32 [16], replicated, may hold values from 1 to 32, as said below
- stored_address_tensor: bfloat16 [2, 16, 32, 1024], P('section'), may hold values from -6 to 6
- stored_content_tensor: bfloat16 [2, 16, 32, 1024], P('section'), may hold values from -6 to 6
- layer_scale_factors: bfloat16 [2, 8192], P('section'), may hold values from 0.5 to 1.5
- question_matrix: bfloat16 [2, 8192, 8192], P('section', None, 'tp'), may hold values from -0.0625 to 0.0625
- address_content_matrix: bfloat16 [2, 8192, 2048], P('section'), may hold values from -0.0625 to 0.0625
- projection_back_matrix: bfloat16 [2, 8192, 8192], P('section', 'tp'), may hold values from -0.0625 to 0.0625
- ending_scale_factors: bfloat16 [8192], replicated, may hold values from 0.5 to 1.5
- lexicon_matrix: bfloat16 [32768, 8192], P(('section', 'tp')), may hold values from -0.1875 to 0.1875
- sampling_warmth: float32 [16], replicated, may hold values from 0.6 to 1.4
- sampling_noise: float32 [16, 32768], P(None, ('section', 'tp')), as said below
Outputs:
- new_entries: bfloat16 [2, 16, 2048], P('section', None, 'tp')
- final_hidden: bfloat16 [16, 8192], replicated
- top_score: float32 [16], replicated
- log_norm: float32 [16], replicated
Inputs may be any that keep to these rules, and one draw needn't show every extreme that they name: Slot j continues old slot parent_positions[j]; an old slot may be named several times or not at all. `filled_extents`: some old slot has exactly 32 filled slots and some exactly one. `sampling_noise`: standard Gumbel noise.
All inputs are finite; a program needn't handle non-finite values.
Results may differ from a plain program's by a relative error of at most 0.013.
Values may be sent and summed in bfloat16 or wider, within the bound.
No kernel may reach another device: no remote copies, remote signals or barrier semaphores. Data moves between devices by JAX's collectives and lax.ppermute only.
A program may use at most 128 MiB of HBM per device.

v0:
```python
import jax
import jax.numpy as jnp
from jax import lax
from jax.sharding import PartitionSpec as P

HEAD = 128
KV_HEADS = 8
MICRO = 4


epsilon = 1e-05


def from_behind(value, axis, steps):
    count = lax.axis_size(axis)
    first, last = (max(0, -steps), min(count, count - steps))
    return lax.ppermute(value, axis, [(source, source + steps) for source in range(first, last)])


def from_root(block, axis, source):
    block = jnp.where(lax.axis_index(axis) == source, block, jnp.zeros_like(block))
    return lax.psum(block, axis)


def scaled_rows(hidden_f, gain_row):
    return (hidden_f * gain_row.astype(jnp.float32)).astype(jnp.bfloat16)


def grouped_mixing(
    queries, new_key, new_value, stored_address_lines, stored_content_lines, extent_each_line
):
    row_count = queries.shape[0]
    slot_count = stored_address_lines.shape[1]
    score_scale = HEAD ** (-0.5)
    scores = (
        jnp.einsum("nd,ncd->nc", queries, stored_address_lines, preferred_element_type=jnp.float32)
        * score_scale
    )
    own_score = (
        jnp.sum(queries.astype(jnp.float32) * new_key.astype(jnp.float32), axis=1) * score_scale
    )
    visible = (
        lax.broadcasted_iota(jnp.int32, (row_count, slot_count), 1) < extent_each_line[:, None]
    )
    highest = jnp.maximum(jnp.max(jnp.where(visible, scores, -1e30), axis=1), own_score)
    weights = jnp.where(visible, jnp.exp(scores - highest[:, None]), 0.0)
    own_weight = jnp.exp(own_score - highest)
    denominator = jnp.sum(weights, axis=1) + own_weight
    weights_bf = (weights / denominator[:, None]).astype(jnp.bfloat16)
    own_prob = (own_weight / denominator).astype(jnp.bfloat16)
    combined = jnp.einsum(
        "nc,ncd->nd", weights_bf, stored_content_lines, preferred_element_type=jnp.float32
    )
    combined = combined + own_prob.astype(jnp.float32)[:, None] * new_value.astype(jnp.float32)
    return combined.astype(jnp.bfloat16)


def head_attend(
    projected,
    share_offset,
    share_width,
    stored_address_lines,
    stored_content_lines,
    extent_each_line,
):
    queries = projected[:, :HEAD].astype(jnp.bfloat16)
    own_pair = projected[:, HEAD:].astype(jnp.bfloat16)
    mixed_result = grouped_mixing(
        queries,
        own_pair[:, :HEAD],
        own_pair[:, HEAD:],
        stored_address_lines,
        stored_content_lines,
        extent_each_line,
    )
    pair_share = lax.dynamic_slice_in_dim(own_pair, share_offset, share_width, 1)
    return (mixed_result, pair_share)


def layer_full(
    carried,
    share_offset,
    share_width,
    gain_row,
    w_project,
    w_output,
    stored_address_lines,
    stored_content_lines,
    extent_each_line,
):
    hidden_f = carried.astype(jnp.float32)
    inverse = lax.rsqrt(jnp.mean(hidden_f * hidden_f, axis=1) + epsilon)
    projected = (
        jnp.dot(scaled_rows(hidden_f, gain_row), w_project, preferred_element_type=jnp.float32)
        * inverse[:, None]
    )
    mixed_result, new_entry = head_attend(
        projected,
        share_offset,
        share_width,
        stored_address_lines,
        stored_content_lines,
        extent_each_line,
    )
    partial_terms = jnp.dot(mixed_result, w_output, preferred_element_type=jnp.float32)
    summed_terms = lax.psum(partial_terms, "tp")
    return ((hidden_f + summed_terms).astype(jnp.bfloat16), new_entry)


def per_device(
    incoming_hidden_states,
    parent_positions,
    filled_extents,
    stored_address_tensor,
    stored_content_tensor,
    layer_scale_factors,
    question_matrix,
    address_content_matrix,
    projection_back_matrix,
    ending_scale_factors,
    lexicon_matrix,
    sampling_warmth,
    sampling_noise,
):
    heads_per_group = lax.axis_size("tp") // KV_HEADS
    group_index = lax.axis_index("tp") // heads_per_group
    pair_width = address_content_matrix.shape[2]
    share_width = pair_width // lax.axis_size("tp")
    share_offset = lax.axis_index("tp") % heads_per_group * share_width
    grouped_addresses = lax.dynamic_slice_in_dim(
        stored_address_tensor[0], group_index * HEAD, HEAD, 2
    )
    grouped_contents = lax.dynamic_slice_in_dim(
        stored_content_tensor[0], group_index * HEAD, HEAD, 2
    )
    stored_address_lines = grouped_addresses[parent_positions]
    stored_content_lines = grouped_contents[parent_positions]
    extent_each_line = filled_extents[parent_positions]
    gain_row = layer_scale_factors[0]
    group_pair_weight = lax.dynamic_slice_in_dim(
        address_content_matrix[0], group_index * 2 * HEAD, 2 * HEAD, 1
    )
    w_project = jnp.concatenate([question_matrix[0], group_pair_weight], axis=1)
    w_output = projection_back_matrix[0]
    segment_index = lax.axis_index("section")
    segment_count = lax.axis_size("section")
    all_rows = incoming_hidden_states.shape[0]
    micro_count = MICRO
    per_micro = all_rows // micro_count
    carried_start = jnp.zeros((per_micro, incoming_hidden_states.shape[1]), jnp.bfloat16)
    entries_start = jnp.zeros((all_rows, share_width), jnp.bfloat16)
    finals_start = jnp.zeros((all_rows, incoming_hidden_states.shape[1]), jnp.bfloat16)

    def tick(tick_index, state_tuple):
        carried, entries, finals = state_tuple
        offset = tick_index - segment_index
        active = (offset >= 0) & (offset < micro_count)
        row_start = jnp.clip(offset, 0, micro_count - 1) * per_micro
        incoming = lax.dynamic_slice_in_dim(
            incoming_hidden_states,
            jnp.clip(tick_index, 0, micro_count - 1) * per_micro,
            per_micro,
            0,
        )
        inputs = jnp.where(segment_index == 0, incoming, carried)
        block_keys = lax.dynamic_slice_in_dim(stored_address_lines, row_start, per_micro, 0)
        block_values = lax.dynamic_slice_in_dim(stored_content_lines, row_start, per_micro, 0)
        block_lengths = lax.dynamic_slice_in_dim(extent_each_line, row_start, per_micro, 0)
        output, new_entry = layer_full(
            inputs,
            share_offset,
            share_width,
            gain_row,
            w_project,
            w_output,
            block_keys,
            block_values,
            block_lengths,
        )
        entries = jnp.where(
            active, lax.dynamic_update_slice_in_dim(entries, new_entry, row_start, 0), entries
        )
        finals = jnp.where(
            active & (segment_index == segment_count - 1),
            lax.dynamic_update_slice_in_dim(finals, output, row_start, 0),
            finals,
        )
        carried = from_behind(output, "section", 1)
        return (carried, entries, finals)

    carried, entries, finals = lax.fori_loop(
        0, segment_count + micro_count - 1, tick, (carried_start, entries_start, finals_start)
    )
    final_rows = from_root(finals, "section", segment_count - 1)
    final_f = final_rows.astype(jnp.float32)
    inverse = lax.rsqrt(jnp.mean(final_f * final_f, axis=1) + epsilon)
    lexicon_scores = (
        jnp.einsum(
            "rd,vd->rv",
            scaled_rows(final_f, ending_scale_factors),
            lexicon_matrix,
            preferred_element_type=jnp.float32,
        )
        * inverse[:, None]
    )
    divided_scores = lexicon_scores / sampling_warmth[:, None]
    noisy_best = jnp.max(divided_scores + sampling_noise, axis=1)
    peak_value = jnp.max(divided_scores, axis=1)
    mass_total = jnp.sum(jnp.exp(divided_scores - peak_value[:, None]), axis=1)
    best_score, peak_all = lax.pmax((noisy_best, peak_value), ("section", "tp"))
    mass_all = lax.psum(mass_total * jnp.exp(peak_value - peak_all), ("section", "tp"))
    log_norm = peak_all + jnp.log(mass_all)
    return (entries.reshape(1, all_rows, share_width), final_rows, best_score, log_norm)


def solution(mesh):
    in_specs = (
        P(),
        P(),
        P(),
        P("section", None, None, None),
        P("section", None, None, None),
        P("section", None),
        P("section", None, "tp"),
        P("section", None, None),
        P("section", "tp", None),
        P(),
        P(("section", "tp"), None),
        P(),
        P(None, ("section", "tp")),
    )
    out_specs = (P("section", None, "tp"), P(), P(), P())
    return jax.shard_map(
        per_device, mesh=mesh, in_specs=in_specs, out_specs=out_specs, check_vma=False
    )
```

profile of v0, /device:TPU:1, one launch (start us, length us, event | category | flops | bytes accessed | tf_op | source)
XLA Modules:
  0.0 847.4 jit_solution(16817780674609550002)
XLA Ops:
  8.0 0.7 compare_select_fusion
  8.7 1.0 dynamic-slice_bitcast_fusion.1
  10.9 0.7 gather_fusion
  11.6 2.6 dynamic-slice_bitcast_fusion
  14.4 3.5 pad_maximum_fusion
  18.1 662.0 %while.19 = (s32[]{:T(128)}, bf16[4,8192]{1,0:T(4,128)(2,1)S(1)}, bf16[16,32]{1,0:T(8,128)(2,1)S(1)}, bf16[16,8192]{1,0:T(8,128)(2,1)S(1)}, pred[]{:T(512)}, /*i...) while((s32[]{:T(128)}, bf16[4,8192]{1,0:T(4,128)(2,1)S(1)}, ...), condition=%wide.region_6.7_spmd, body=%wide.region_0.6_spmd.sunk | while | flops 34030128 | bytes 10396708 | solution.py:191
  18.2 1.1 fusion.52
  19.3 3.7 fusion.53
  23.9 1.1 fusion.58
  25.1 124.5 %all-reduce.6.cloned.1.call-done = f32[4,8192]{1,0:T(4,128)} async-done(((f32[4,8192]{1,0:T(4,128)}), f32[4,8192]{1,0:T(4,128)}) %all-reduce.6.cloned.1.call-update) | async-done | bytes 131088 | tf_op jit(solution)/shard_map/while/body/eval_jaxpr/psum | solution.py:106
  149.6 1.0 select_dynamic-update-slice_fusion.2
  150.6 1.3 collective-permute-start
  152.0 3.1 collective-permute-done
  155.2 1.1 fusion.52
  156.3 3.7 fusion.53
  160.9 1.1 fusion.58
  162.1 118.8 %all-reduce.6.cloned.1.call-done = f32[4,8192]{1,0:T(4,128)} async-done(((f32[4,8192]{1,0:T(4,128)}), f32[4,8192]{1,0:T(4,128)}) %all-reduce.6.cloned.1.call-update) | async-done | bytes 131088 | tf_op jit(solution)/shard_map/while/body/eval_jaxpr/psum | solution.py:106
  280.8 1.0 select_dynamic-update-slice_fusion.2
  281.8 1.3 collective-permute-start
  283.2 3.1 collective-permute-done
  286.4 1.1 fusion.52
  287.5 3.7 fusion.53
  292.2 1.1 fusion.58
  293.3 118.8 %all-reduce.6.cloned.1.call-done = f32[4,8192]{1,0:T(4,128)} async-done(((f32[4,8192]{1,0:T(4,128)}), f32[4,8192]{1,0:T(4,128)}) %all-reduce.6.cloned.1.call-update) | async-done | bytes 131088 | tf_op jit(solution)/shard_map/while/body/eval_jaxpr/psum | solution.py:106
  412.1 1.0 select_dynamic-update-slice_fusion.2
  413.1 1.3 collective-permute-start
  414.4 3.1 collective-permute-done
  417.6 1.1 fusion.52
  418.7 3.7 fusion.53
  423.4 1.1 fusion.58
  424.5 118.8 %all-reduce.6.cloned.1.call-done = f32[4,8192]{1,0:T(4,128)} async-done(((f32[4,8192]{1,0:T(4,128)}), f32[4,8192]{1,0:T(4,128)}) %all-reduce.6.cloned.1.call-update) | async-done | bytes 131088 | tf_op jit(solution)/shard_map/while/body/eval_jaxpr/psum | solution.py:106
  543.3 1.0 select_dynamic-update-slice_fusion.2
  544.3 1.3 collective-permute-start
  545.7 3.1 collective-permute-done
  548.8 1.1 fusion.52
  549.9 3.7 fusion.53
  554.6 1.1 fusion.58
  555.7 118.8 %all-reduce.6.cloned.1.call-done = f32[4,8192]{1,0:T(4,128)} async-done(((f32[4,8192]{1,0:T(4,128)}), f32[4,8192]{1,0:T(4,128)}) %all-reduce.6.cloned.1.call-update) | async-done | bytes 131088 | tf_op jit(solution)/shard_map/while/body/eval_jaxpr/psum | solution.py:106
  674.5 1.0 select_dynamic-update-slice_fusion.2
  675.5 1.3 collective-permute-start
  676.9 3.1 collective-permute-done
  680.0 0.7 broadcast_select_fusion
  680.8 24.1 %all-reduce.4.cloned.1.call-done = bf16[16,8192]{1,0:T(8,128)(2,1)} async-done(((bf16[16,8192]{1,0:T(8,128)(2,1)}), bf16[16,8192]{1,0:T(8,128)(2,1)}) %all-reduce.4.cloned.1.call-update) | async-done | bytes 262160 | tf_op jit(solution)/shard_map/psum | solution.py:22
  704.9 1.2 fusion.22
  706.1 3.6 fusion.27
  709.9 66.6 %all-reduce = (f32[16]{0:T(128)}, f32[16]{0:T(128)S(1)}) all-reduce(f32[16]{0:T(128)S(1)} %get-tuple-element.317, f32[16]{0:T(128)S(1)} %get-tuple-element.358), channel_id=1, replica_groups=mesh['section'=2,'tp'=64] {'section','tp'}, use_global_device_ids=true, to_apply=%region_10.11 | all-reduce | flops 32 | bytes 256 | tf_op jit(solution)/shard_map/pmax | solution.py:210
  776.4 62.6 %psum.28 = f32[16]{0:T(128)S(1)} all-reduce(f32[16]{0:T(128)S(1)} %exponential_multiply_fusion), channel_id=1, replica_groups=mesh['section'=2,'tp'=64] {'section','tp'}, use_global_device_ids=true, to_apply=%region_14.15 | all-reduce | flops 16 | bytes 128 | tf_op jit(solution)/shard_map/psum | solution.py:211
  839.6 0.7 copy.45
  (112 shorter events, 7.6 us)
Async XLA Ops:
  8.0 2.9 copy-start
  11.5 2.9 copy-start.3
  14.4 3.5 copy-start.4
  14.4 3.6 copy-start.1
  18.1 662.7 %copy-start.6 = (bf16[8192]{0:T(1024)(128)(2,1)S(1)}, bf16[8192]{0:T(1024)(128)(2,1)}, u32[]{:S(2)}) copy-start(bf16[8192]{0:T(1024)(128)(2,1)} %param.24) | copy-start | bytes 49156
  18.1 688.0 %copy-start.8 = (f32[16]{0:T(128)S(1)}, f32[16]{0:T(128)}, u32[]{:S(2)}) copy-start(f32[16]{0:T(128)} %param.26) | copy-start | bytes 196
  18.1 131.5 %all-reduce.6.cloned.1.call-start = ((), (), s32[]{:S(2)}) async-start(), calls=%async_computation.1 | async-start | bytes 262144 | tf_op jit(solution)/shard_map/while/body/eval_jaxpr/psum | solution.py:106
  150.6 4.5 collective-permute-start
  155.2 125.7 %all-reduce.6.cloned.1.call-start = ((), (), s32[]{:S(2)}) async-start(), calls=%async_computation.1 | async-start | bytes 262144 | tf_op jit(solution)/shard_map/while/body/eval_jaxpr/psum | solution.py:106
  281.8 4.5 collective-permute-start
  286.4 125.7 %all-reduce.6.cloned.1.call-start = ((), (), s32[]{:S(2)}) async-start(), calls=%async_computation.1 | async-start | bytes 262144 | tf_op jit(solution)/shard_map/while/body/eval_jaxpr/psum | solution.py:106
  413.1 4.5 collective-permute-start
  417.6 125.7 %all-reduce.6.cloned.1.call-start = ((), (), s32[]{:S(2)}) async-start(), calls=%async_computation.1 | async-start | bytes 262144 | tf_op jit(solution)/shard_map/while/body/eval_jaxpr/psum | solution.py:106
  544.3 4.5 collective-permute-start
  548.8 125.7 %all-reduce.6.cloned.1.call-start = ((), (), s32[]{:S(2)}) async-start(), calls=%async_computation.1 | async-start | bytes 262144 | tf_op jit(solution)/shard_map/while/body/eval_jaxpr/psum | solution.py:106
  675.5 4.5 collective-permute-start
  680.0 160.3 %copy-start.5 = (bf16[16,32]{1,0:T(8,128)(2,1)}, bf16[16,32]{1,0:T(8,128)(2,1)S(1)}, u32[]{:S(2)}) copy-start(bf16[16,32]{1,0:T(8,128)(2,1)S(1)} %get-tuple-element.314) | copy-start | bytes 3076
  680.0 29.6 %copy-start.7 = (f32[16,256]{1,0:T(8,128)S(1)}, f32[16,256]{1,0:T(8,128)}, u32[]{:S(2)}) copy-start(f32[16,256]{1,0:T(8,128)} %param.27) | copy-start | bytes 49156
  680.0 24.8 %all-reduce.4.cloned.1.call-start = ((), (), s32[]{:S(2)}) async-start(), calls=%async_computation | async-start | bytes 524288 | tf_op jit(solution)/shard_map/psum | solution.py:22
  704.9 134.7 %copy-start.2 = (bf16[16,8192]{1,0:T(8,128)(2,1)S(1)}, bf16[16,8192]{1,0:T(8,128)(2,1)}, u32[]{:S(2)}) copy-start(bf16[16,8192]{1,0:T(8,128)(2,1)} %all-reduce.4.cloned.1.call-done) | copy-start | bytes 786436
Sparse Core Ops, SparseCore 0:
  25.2 124.3 all-reduce.5
  162.2 118.6 all-reduce.5
  293.4 118.6 all-reduce.5
  424.6 118.6 all-reduce.5
  555.8 118.6 all-reduce.5
Sparse Core Ops, SparseCore 1:
  683.5 21.3 all-reduce.3
where the time goes:
time: 848 us; the launch traced here: 847 us
  waiting for transfers between devices  639 us (75%)
  blocking collectives  129 us (15%)
  matrix products  28.8 us (3%)
  other arithmetic  20.8 us (2%)
  between operations  15.3 us (2%)
    psum x5, waiting for transfers between devices, layer_full(): summed_terms = lax.psum(partial_terms, 'tp')  600 us
    pmax x1, blocking collectives, per_device(): best_score, peak_all = lax.pmax((noisy_best, peak_value), ('section', 'tp'))  66.6 us
    psum x1, blocking collectives, per_device(): lax.psum(mass_total * jnp.exp(peak_value - peak_all), ('section', 'tp'))  62.6 us
    psum x1, waiting for transfers between devices, from_root(): return lax.psum(block, axis)  24.1 us
    dot_general x5, matrix products, layer_full(): jnp.dot(scaled_rows(hidden_f, gain_row), w_project, preferred_element_typ...  18.5 us
  transfers between devices with their start and end apart: 11, of which 11 were waited for; matrix products, arithmetic and copies ran while one was open for 0% of the time, Pallas kernels for 0%

commit v1 on v0

v1 whole, which is shorter than its diff:
```python
import jax
import jax.numpy as jnp
from jax import lax
from jax.sharding import PartitionSpec as P

HEAD = 128
KV_HEADS = 8


epsilon = 1e-05


def scaled_rows(hidden_f, gain_row):
    return (hidden_f * gain_row.astype(jnp.float32)).astype(jnp.bfloat16)


def grouped_mixing(
    queries, new_key, new_value, stored_address_lines, stored_content_lines, extent_each_line
):
    row_count = queries.shape[0]
    slot_count = stored_address_lines.shape[1]
    score_scale = HEAD ** (-0.5)
    scores = (
        jnp.einsum("nd,ncd->nc", queries, stored_address_lines, preferred_element_type=jnp.float32)
        * score_scale
    )
    own_score = (
        jnp.sum(queries.astype(jnp.float32) * new_key.astype(jnp.float32), axis=1) * score_scale
    )
    visible = (
        lax.broadcasted_iota(jnp.int32, (row_count, slot_count), 1) < extent_each_line[:, None]
    )
    highest = jnp.maximum(jnp.max(jnp.where(visible, scores, -1e30), axis=1), own_score)
    weights = jnp.where(visible, jnp.exp(scores - highest[:, None]), 0.0)
    own_weight = jnp.exp(own_score - highest)
    denominator = jnp.sum(weights, axis=1) + own_weight
    weights_bf = (weights / denominator[:, None]).astype(jnp.bfloat16)
    own_prob = (own_weight / denominator).astype(jnp.bfloat16)
    combined = jnp.einsum(
        "nc,ncd->nd", weights_bf, stored_content_lines, preferred_element_type=jnp.float32
    )
    combined = combined + own_prob.astype(jnp.float32)[:, None] * new_value.astype(jnp.float32)
    return combined.astype(jnp.bfloat16)


def per_device(
    incoming_hidden_states,
    parent_positions,
    filled_extents,
    stored_address_tensor,
    stored_content_tensor,
    layer_scale_factors,
    question_matrix,
    address_content_matrix,
    projection_back_matrix,
    ending_scale_factors,
    lexicon_matrix,
    sampling_warmth,
    sampling_noise,
):
    shards = lax.axis_size("tp")
    sections = lax.axis_size("section")
    shard = lax.axis_index("tp")
    section = lax.axis_index("section")
    heads_per_group = shards // KV_HEADS
    group_index = shard // heads_per_group
    pair_width = address_content_matrix.shape[2]
    share_width = pair_width // shards
    share_offset = shard % heads_per_group * share_width
    rows, width = incoming_hidden_states.shape
    chunk = width // shards
    grouped_addresses = lax.dynamic_slice_in_dim(
        stored_address_tensor[0], group_index * HEAD, HEAD, 2
    )
    grouped_contents = lax.dynamic_slice_in_dim(
        stored_content_tensor[0], group_index * HEAD, HEAD, 2
    )
    stored_address_lines = grouped_addresses[parent_positions]
    stored_content_lines = grouped_contents[parent_positions]
    extent_each_line = filled_extents[parent_positions]
    gain_row = layer_scale_factors[0]
    group_pair_weight = lax.dynamic_slice_in_dim(
        address_content_matrix[0], group_index * 2 * HEAD, 2 * HEAD, 1
    )
    w_output = projection_back_matrix[0]

    def layer(hidden):
        hidden_f = hidden.astype(jnp.float32)
        inverse = lax.rsqrt(jnp.mean(hidden_f * hidden_f, axis=1) + epsilon)[:, None]
        scaled = scaled_rows(hidden_f, gain_row)
        queries = jnp.dot(scaled, question_matrix[0], preferred_element_type=jnp.float32) * inverse
        pair = jnp.dot(scaled, group_pair_weight, preferred_element_type=jnp.float32) * inverse
        pair = pair.astype(jnp.bfloat16)
        mixed = grouped_mixing(
            queries.astype(jnp.bfloat16),
            pair[:, :HEAD],
            pair[:, HEAD:],
            stored_address_lines,
            stored_content_lines,
            extent_each_line,
        )
        entry = lax.dynamic_slice_in_dim(pair, share_offset, share_width, 1)
        terms = jnp.dot(mixed, w_output, preferred_element_type=jnp.float32).astype(jnp.bfloat16)
        terms = terms.reshape(rows, shards, chunk).transpose(1, 0, 2)
        terms = lax.all_to_all(terms, "tp", 0, 0)
        summed = jnp.sum(terms.astype(jnp.float32), axis=0)
        own = lax.dynamic_slice_in_dim(hidden, shard * chunk, chunk, 1)
        return (own.astype(jnp.float32) + summed).astype(jnp.bfloat16), entry

    def spread(block, source):
        copies = jnp.broadcast_to(block, (sections * shards, rows, chunk))
        blocks = lax.all_to_all(copies, ("section", "tp"), 0, 0)
        blocks = blocks[source * shards : (source + 1) * shards]
        return blocks.transpose(1, 0, 2).reshape(rows, width)

    block, first_entry = layer(incoming_hidden_states)
    block, entry = layer(spread(block, 0))
    final_rows = spread(block, 1)
    entry = jnp.where(section == 0, first_entry, entry)

    final_f = final_rows.astype(jnp.float32)
    inverse = lax.rsqrt(jnp.mean(final_f * final_f, axis=1) + epsilon)
    lexicon_scores = (
        jnp.einsum(
            "rd,vd->rv",
            scaled_rows(final_f, ending_scale_factors),
            lexicon_matrix,
            preferred_element_type=jnp.float32,
        )
        * inverse[:, None]
    )
    divided_scores = lexicon_scores / sampling_warmth[:, None]
    noisy_best = jnp.max(divided_scores + sampling_noise, axis=1)
    peak_value = jnp.max(divided_scores, axis=1)
    mass_total = jnp.sum(jnp.exp(divided_scores - peak_value[:, None]), axis=1)
    stats = jnp.concatenate([noisy_best, peak_value, mass_total, jnp.zeros((128 - 3 * rows,), jnp.float32)])
    stats = jnp.broadcast_to(stats, (sections * shards, 1, 128))
    stats = lax.all_to_all(stats, ("section", "tp"), 0, 0)[:, 0]
    best_score = jnp.max(stats[:, :rows], axis=0)
    peaks = stats[:, rows : 2 * rows]
    peak_all = jnp.max(peaks, axis=0)
    mass_all = jnp.sum(stats[:, 2 * rows : 3 * rows] * jnp.exp(peaks - peak_all), axis=0)
    log_norm = peak_all + jnp.log(mass_all)
    return (entry[None], final_rows, best_score, log_norm)


def solution(mesh):
    in_specs = (
        P(),
        P(),
        P(),
        P("section", None, None, None),
        P("section", None, None, None),
        P("section", None),
        P("section", None, "tp"),
        P("section", None, None),
        P("section", "tp", None),
        P(),
        P(("section", "tp"), None),
        P(),
        P(None, ("section", "tp")),
    )
    out_specs = (P("section", None, "tp"), P(), P(), P())
    return jax.shard_map(
        per_device, mesh=mesh, in_specs=in_specs, out_specs=out_specs, check_vma=False
    )
```

time: 848 us -> 114 us (0.13)
  waiting for transfers between devices: 639 us -> 41.5 us
  blocking collectives: 129 us -> 18.8 us
  starting transfers between devices: 6.5 us -> 26.4 us
  matrix products: 28.8 us -> 12.2 us
  between operations: 15.3 us -> 0.98 us
  other arithmetic: 20.8 us -> 6.51 us
    psum x6 -> x0, waiting for transfers between devices: 624 us -> none  [the longest x5 600 us: layer_full(): summed_terms = lax.psum(partial_terms, 'tp')]
    pmax x1 -> x0, blocking collectives: 66.6 us -> none  [per_device(): best_score, peak_all = lax.pmax((noisy_best, peak_value), ('section', 'tp'))]
    psum x1 -> x0, blocking collectives: 62.6 us -> none  [per_device(): lax.psum(mass_total * jnp.exp(peak_value - peak_all), ('section', 'tp'))]
    all_to_all x0 -> x4, waiting for transfers between devices: none -> 41.5 us  [the longest x2 19 us: layer(): terms = lax.all_to_all(terms, 'tp', 0, 0)]
    all_to_all x0 -> x4, starting transfers between devices: none -> 26.4 us  [the longest x2 16.7 us: layer(): terms = lax.all_to_all(terms, 'tp', 0, 0)]
    all_to_all x0 -> x1, blocking collectives: none -> 18.8 us  [spread(): blocks = lax.all_to_all(copies, ('section', 'tp'), 0, 0)]
    dot_general x10 -> x6, matrix products: 24 us -> 7.9 us  [the longest x2 5.99 us: layer(): jnp.dot(scaled, group_pair_weight, preferred_element_type=jnp.float32)]
    ppermute x5 -> x0, waiting for transfers between devices: 15.7 us -> none  [from_behind(): lax.ppermute(value, axis, [(source, source + steps) for source in range(f...]
  transfers between devices with their start and end apart: 11 -> 4, of which waited for: 11 -> 4; matrix products, arithmetic and copies ran while one was open for 0% -> 1% of each run, Pallas kernels for 0% -> 0%
where the time goes in v1:
time: 114 us; the launch traced here: 113 us
  waiting for transfers between devices  41.5 us (36%)
  starting transfers between devices  26.4 us (23%)
  blocking collectives  18.8 us (16%)
  matrix products  12.2 us (11%)
  local copies, waits for them, and re-layouts  6.79 us (6%)
  other arithmetic  6.51 us (6%)
    all_to_all x2, waiting for transfers between devices, layer(): terms = lax.all_to_all(terms, 'tp', 0, 0)  19 us
    all_to_all x1, blocking collectives, spread(): blocks = lax.all_to_all(copies, ('section', 'tp'), 0, 0)  18.8 us
    all_to_all x2, starting transfers between devices, layer(): terms = lax.all_to_all(terms, 'tp', 0, 0)  16.7 us
    all_to_all x1, waiting for transfers between devices, spread(): blocks = lax.all_to_all(copies, ('section', 'tp'), 0, 0)  13.6 us
    all_to_all x1, waiting for transfers between devices, per_device(): stats = lax.all_to_all(stats, ('section', 'tp'), 0, 0)[:, 0]  8.94 us
    dot_general x2, matrix products, layer(): jnp.dot(scaled, group_pair_weight, preferred_element_type=jnp.float32)  5.99 us
    all_to_all x1, starting transfers between devices, spread(): blocks = lax.all_to_all(copies, ('section', 'tp'), 0, 0)  5.47 us
    all_to_all x1, starting transfers between devices, per_device(): stats = lax.all_to_all(stats, ('section', 'tp'), 0, 0)[:, 0]  4.21 us
  transfers between devices with their start and end apart: 4, of which 4 were waited for; matrix products, arithmetic and copies ran while one was open for 1% of the time, Pallas kernels for 0%

profile of v1, /device:TPU:1, one launch (start us, length us, event | category | flops | bytes accessed | tf_op | source)
XLA Modules:
  0.0 113.2 jit_solution(17350122473430401190)
XLA Ops:
  0.7 0.8 compare_select_fusion
  1.5 0.8 convert_element_type.131
  2.3 1.1 fusion.44
  3.4 1.0 dynamic-slice_bitcast_fusion
  4.4 0.6 gather_fusion.1
  5.0 1.3 %gather_fusion = s32[16]{0:T(128)S(1)} fusion(s32[16]{0:T(128)} %param.15, s32[1024]{0:T(1024)S(1)} %pad_clamp_fusion), kind=kCustom, calls=%fused_computation | custom fusion | bytes 192 | tf_op jit(solution)/shard_map/gather | solution.py:80
  6.3 3.0 %fusion.28 = bf16[16,256]{1,0:T(8,128)(2,1)S(1)} fusion(bf16[1,8192,2048]{2,1,0:T(8,128)(2,1)} %param.20, s32[]{:T(128)S(6)} %select_n.54, bf16[16,8192]{1,0:T(8,128)(2,1)} %param.13, f32[8192]{0:T(1024)S(1)} %bitcast.107, f32[16]{0:T(128)S(1)} %add_rsqrt_fusion.2), kind=kOutput, calls=%fused_computation.24 | convolution fusion | flops 67510272 | bytes 4497476 | tf_op jit(solution)/shard_map/dot_general | solution.py:92
  9.4 0.5 multiply_reduce_fusion.2
  9.9 0.2 fusion.62
  10.1 0.2 select_reduce_fusion.1
  10.3 0.2 fusion.64
  10.5 0.1 fusion.70
  10.6 0.6 gather_fusion.2
  11.2 0.1 fusion.60
  11.4 0.4 fusion.12
  11.8 0.8 copy.79
  12.6 12.0 %all-to-all-start = ((bf16[64,16,128]{2,1,0:T(8,128)(2,1)}), bf16[64,16,128]{2,1,0:T(8,128)(2,1)S(1)}, u32[]{:S(2)}, u32[]{:S(2)}) async-start(bf16[64,16,128]{2,1,0:T(8,128)(2,1)} %bitcast.106), calls=%async_computation | async-start | bytes 524288 | tf_op jit(solution)/shard_map/all_to_all | solution.py:105
  24.5 9.5 %all-to-all-done = bf16[64,16,128]{2,1,0:T(8,128)(2,1)S(1)} async-done(((bf16[64,16,128]{2,1,0:T(8,128)(2,1)}), bf16[64,16,128]{2,1,0:T(8,128)(2,1)S(1)}, u32[]{:S(2)}, u32[]{:S(2)}) %all-to-all-start) | async-done | bytes 262176 | tf_op jit(solution)/shard_map/all_to_all | solution.py:105
  34.0 0.1 convert_reduce_fusion.1
  34.1 0.1 broadcast_in_dim.24
  34.2 18.8 %all_to_all.25 = bf16[128,16,128]{2,1,0:T(8,128)(2,1)S(1)} all-to-all(bf16[128,16,128]{2,1,0:T(8,128)(2,1)S(1)} %broadcast_in_dim.24), channel_id=1, replica_groups=mesh['section'=2,'tp'=64] {'section','tp'}, dimensions={0} | all-to-all | bytes 1048576 | tf_op jit(solution)/shard_map/all_to_all | solution.py:112
  53.0 0.2 fusion.46
  53.3 3.0 %fusion.25 = bf16[16,256]{1,0:T(8,128)(2,1)S(1)} fusion(bf16[1,8192,2048]{2,1,0:T(8,128)(2,1)} %param.20, s32[]{:T(128)S(6)} %select_n.54, bf16[64,2,8,128]{3,2,1,0:T(8,128)(2,1)S(1)} %get-tuple-element.9, f32[16]{0:T(128)S(1)} %add_rsqrt_fusion.1), kind=kOutput, calls=%fused_computation.23 | convolution fusion | flops 67117056 | bytes 4464708 | tf_op jit(solution)/shard_map/dot_general | solution.py:92
  56.2 0.5 multiply_reduce_fusion.1
  56.8 0.2 fusion.58
  57.0 0.2 select_reduce_fusion
  57.2 0.2 fusion.65
  57.4 0.1 fusion.71
  57.5 0.1 fusion.56
  57.6 0.4 fusion.15
  58.1 0.8 copy.78
  58.8 4.8 %all-to-all-start.2 = ((bf16[64,16,128]{2,1,0:T(8,128)(2,1)}), bf16[64,16,128]{2,1,0:T(8,128)(2,1)S(1)}, u32[]{:S(2)}, u32[]{:S(2)}) async-start(bf16[64,16,128]{2,1,0:T(8,128)(2,1)} %bitcast.104), calls=%async_computation.2 | async-start | bytes 524288 | tf_op jit(solution)/shard_map/all_to_all | solution.py:105
  63.6 9.5 %all-to-all-done.2 = bf16[64,16,128]{2,1,0:T(8,128)(2,1)S(1)} async-done(((bf16[64,16,128]{2,1,0:T(8,128)(2,1)}), bf16[64,16,128]{2,1,0:T(8,128)(2,1)S(1)}, u32[]{:S(2)}, u32[]{:S(2)}) %all-to-all-start.2) | async-done | bytes 262176 | tf_op jit(solution)/shard_map/all_to_all | solution.py:105
  73.2 0.9 broadcast_in_dim.26
  74.1 5.5 %all-to-all-start.3 = ((bf16[128,16,128]{2,1,0:T(8,128)(2,1)}), bf16[128,16,128]{2,1,0:T(8,128)(2,1)S(1)}, u32[]{:S(2)}, u32[]{:S(2)}) async-start(bf16[128,16,128]{2,1,0:T(8,128)(2,1)} %broadcast_in_dim.26), calls=%async_computation.3 | async-start | bytes 1048576 | tf_op jit(solution)/shard_map/all_to_all | solution.py:112
  79.6 13.6 %all-to-all-done.3 = bf16[128,16,128]{2,1,0:T(8,128)(2,1)S(1)} async-done(((bf16[128,16,128]{2,1,0:T(8,128)(2,1)}), bf16[128,16,128]{2,1,0:T(8,128)(2,1)S(1)}, u32[]{:S(2)}, u32[]{:S(2)}) %all-to-all-start.3) | async-done | bytes 524320 | tf_op jit(solution)/shard_map/all_to_all | solution.py:112
  93.2 0.2 multiply_reduce_fusion
  93.4 3.6 %fusion.76 = (f32[16]{0:T(128)S(1)}, f32[16,256]{1,0:T(8,128)S(1)}) fusion(f32[16]{0:T(128)S(1)} %copy-done.7, f32[16]{0:T(128)S(1)} %add_rsqrt_fusion, bf16[256,8192]{1,0:T(8,128)(2,1)} %param.23, bf16[16,8192]{1,0:T(8,128)(2,1)S(1)} %copy_bitcast_fusion, f32[8192]{0:T(1024)S(1)} %convert_element_type.163), kind=kOutput, calls=%fused_computation.108 | convolution fusion | flops 67514352 | bytes 4505792 | tf_op jit(solution)/shard_map/rd,vd->rv/dot_general | solution.py:124
  97.1 0.2 add_reduce_fusion
  97.3 0.1 pad_maximum_fusion
  97.3 0.7 broadcast_in_dim.53
  98.0 4.2 %all-to-all-start.4 = ((f32[128,1,128]{2,1,0:T(1,128)}), f32[128,1,128]{2,1,0:T(1,128)S(1)}, u32[]{:S(2)}, u32[]{:S(2)}) async-start(f32[128,1,128]{2,1,0:T(1,128)} %broadcast_in_dim.53), calls=%async_computation.4 | async-start | bytes 131072 | tf_op jit(solution)/shard_map/all_to_all | solution.py:138
  102.2 0.7 select_bitcast_fusion
  102.9 8.9 %all-to-all-done.4 = f32[128,1,128]{2,1,0:T(1,128)S(1)} async-done(((f32[128,1,128]{2,1,0:T(1,128)}), f32[128,1,128]{2,1,0:T(1,128)S(1)}, u32[]{:S(2)}, u32[]{:S(2)}) %all-to-all-start.4) | async-done | bytes 65568 | tf_op jit(solution)/shard_map/all_to_all | solution.py:138
  111.8 0.1 copy.42
  111.9 0.1 slice_reduce_fusion.1
  112.0 0.6 fusion.55
  112.7 0.5 log_add_fusion
  (31 shorter events, 0.3 us)
Async XLA Ops:
  0.6 10.7 %copy-start = (bf16[1,128,8192]{2,1,0:T(8,128)(2,1)S(1)}, bf16[1,128,8192]{2,1,0:T(8,128)(2,1)}, u32[]{:S(2)}) copy-start(bf16[1,128,8192]{2,1,0:T(8,128)(2,1)} %param.21) | copy-start | bytes 6291460
  6.3 3.1 %copy-start.1 = (bf16[1,8192,128]{2,1,0:T(8,128)(2,1)S(1)}, bf16[1,8192,128]{2,1,0:T(8,128)(2,1)}, u32[]{:S(2)}) copy-start(bf16[1,8192,128]{2,1,0:T(8,128)(2,1)} %param.19) | copy-start | bytes 6291460
  6.3 3.1 %copy-start.3 = (bf16[16,8192]{1,0:T(8,128)(2,1)S(1)}, bf16[16,8192]{1,0:T(8,128)(2,1)}, u32[]{:S(2)}) copy-start(bf16[16,8192]{1,0:T(8,128)(2,1)} %param.13) | copy-start | bytes 786436
  12.6 21.5 %all-to-all-start = ((bf16[64,16,128]{2,1,0:T(8,128)(2,1)}), bf16[64,16,128]{2,1,0:T(8,128)(2,1)S(1)}, u32[]{:S(2)}, u32[]{:S(2)}) async-start(bf16[64,16,128]{2,1,0:T(8,128)(2,1)} %bitcast.106), calls=%async_computation | async-start | bytes 524288 | tf_op jit(solution)/shard_map/all_to_all | solution.py:105
  53.3 3.0 %copy-start.2 = (bf16[1,8192,128]{2,1,0:T(8,128)(2,1)S(1)}, bf16[1,8192,128]{2,1,0:T(8,128)(2,1)}, u32[]{:S(2)}) copy-start(bf16[1,8192,128]{2,1,0:T(8,128)(2,1)} %param.19) | copy-start | bytes 6291460
  58.0 21.5 %copy-start.5 = (bf16[8192]{0:T(1024)(128)(2,1)S(1)}, bf16[8192]{0:T(1024)(128)(2,1)}, u32[]{:S(2)}) copy-start(bf16[8192]{0:T(1024)(128)(2,1)} %param.22) | copy-start | bytes 49156
  58.0 35.4 %copy-start.7 = (f32[16]{0:T(128)S(1)}, f32[16]{0:T(128)}, u32[]{:S(2)}) copy-start(f32[16]{0:T(128)} %param.24) | copy-start | bytes 196
  58.8 14.3 %all-to-all-start.2 = ((bf16[64,16,128]{2,1,0:T(8,128)(2,1)}), bf16[64,16,128]{2,1,0:T(8,128)(2,1)S(1)}, u32[]{:S(2)}, u32[]{:S(2)}) async-start(bf16[64,16,128]{2,1,0:T(8,128)(2,1)} %bitcast.104), calls=%async_computation.2 | async-start | bytes 524288 | tf_op jit(solution)/shard_map/all_to_all | solution.py:105
  74.1 19.1 %all-to-all-start.3 = ((bf16[128,16,128]{2,1,0:T(8,128)(2,1)}), bf16[128,16,128]{2,1,0:T(8,128)(2,1)S(1)}, u32[]{:S(2)}, u32[]{:S(2)}) async-start(bf16[128,16,128]{2,1,0:T(8,128)(2,1)} %broadcast_in_dim.26), calls=%async_computation.3 | async-start | bytes 1048576 | tf_op jit(solution)/shard_map/all_to_all | solution.py:112
  93.4 3.6 %copy-start.4 = (bf16[16,8192]{1,0:T(8,128)(2,1)}, bf16[16,8192]{1,0:T(8,128)(2,1)S(1)}, u32[]{:S(2)}) copy-start(bf16[16,8192]{1,0:T(8,128)(2,1)S(1)} %copy_bitcast_fusion) | copy-start | bytes 786436
  93.4 3.6 %copy-start.6 = (f32[16,256]{1,0:T(8,128)S(1)}, f32[16,256]{1,0:T(8,128)}, u32[]{:S(2)}) copy-start(f32[16,256]{1,0:T(8,128)} %param.25) | copy-start | bytes 49156
  98.0 13.8 %all-to-all-start.4 = ((f32[128,1,128]{2,1,0:T(1,128)}), f32[128,1,128]{2,1,0:T(1,128)S(1)}, u32[]{:S(2)}, u32[]{:S(2)}) async-start(f32[128,1,128]{2,1,0:T(1,128)} %broadcast_in_dim.53), calls=%async_computation.4 | async-start | bytes 131072 | tf_op jit(solution)/shard_map/all_to_all | solution.py:138
